TPU v7x, 32 devices: a whole 2x2x4 slice. The times are simulated.
32 devices in a mesh: blk: 4 (over y, x), grp: 8 (over z, core).
Axes of the slice: x: 2, y: 2, z: 4, core: 2. Of those that a mesh axis runs over, the one named last changes fastest.
Arguments:
- picture_vectors_prenorm: float32 [512, 1152], P(('blk', 'grp')), may hold values from -2 to 2, as said below
- caption_vectors_prenorm: float32 [512, 1152], P(('blk', 'grp')), may hold values from -2 to 2, as said below
- matched_caption_ids: int32 [512], P(('blk', 'grp')), may hold values from 0 to 511, each once
- sharpness_coefficient: float32 [1], replicated, may hold values from 4 to 12
- additive_offset_term: float32 [1], replicated, may hold values from -6 to -2
- heads_mixed_concluding: bfloat16 [12288, 1536], P(('blk', 'grp')), may hold values from -6 to 6
- dense_result_adjoint: bfloat16 [12288, 1536], P(('blk', 'grp')), may hold values from -6 to 6
- dense_mapping_matrix: bfloat16 [1536, 1536], P('grp'), may hold values from -0.15625 to 0.15625
Outputs:
- image_grad: float32 [512, 1152], P(('blk', 'grp'))
- text_grad: float32 [512, 1152], P(('blk', 'grp'))
- attn_grad: bfloat16 [12288, 1536], P(('blk', 'grp'))
- weight_grad: float32 [1536, 1536], P('grp')
Inputs may be any that keep to these rules, and one draw needn't show every extreme that they name: `matched_caption_ids`: each text index appears once. `picture_vectors_prenorm`: raw embedding entries. `caption_vectors_prenorm`: raw embedding entries.
All inputs are finite; a program needn't handle non-finite values.
Results may differ from a plain program's by a relative error of at most 0.0053.
Values may be sent and summed in bfloat16 or wider, within the bound.
A program may use at most 128 MiB of HBM per device.

v0:
```python
import math

import jax
import jax.numpy as jnp
from jax import lax
from jax.sharding import PartitionSpec as P

stability_floor = 1e-06


def as_sent(x):

    def short(part):
        return part.astype(jnp.bfloat16) if part.dtype == jnp.float32 else part

    return jax.tree.map(short, x)


def passed_along(x, axis, by):
    peers = lax.axis_size(axis)
    return lax.ppermute(x, axis, [(i, (i + by) % peers) for i in range(peers)])


def unit_rows(raw):
    row_scale = lax.rsqrt(jnp.sum(raw * raw, axis=1, keepdims=True) + stability_floor)
    return (raw * row_scale, row_scale)


def back_through_norm(normed, row_scale, row_grad):
    along_unit = jnp.sum(normed * row_grad, axis=1, keepdims=True)
    return (row_grad - normed * along_unit) * row_scale


def weighted_sum(query_half, key_half, labels, sigmoid_multiplier, bias_value):
    inner_dots = lax.dot_general(
        query_half, key_half, (((1,), (1,)), ((), ())), preferred_element_type=jnp.float32
    )
    logits = sigmoid_multiplier * inner_dots + bias_value
    pair_weights = (sigmoid_multiplier * (jax.nn.sigmoid(logits) - labels)).astype(jnp.bfloat16)
    return jnp.dot(pair_weights, key_half, preferred_element_type=jnp.float32)


def pass_on(held_rows, direction):
    return jax.tree.map(
        lambda part, own: part.astype(own.dtype),
        passed_along(as_sent(held_rows), "blk", direction),
        held_rows,
    )


def per_device(
    picture_vectors_prenorm,
    caption_vectors_prenorm,
    matched_caption_ids,
    sharpness_coefficient,
    additive_offset_term,
    heads_mixed_concluding,
    dense_result_adjoint,
    dense_mapping_matrix,
):
    image_units, image_scale = unit_rows(picture_vectors_prenorm)
    text_units, text_scale = unit_rows(caption_vectors_prenorm)
    image_half = image_units.astype(jnp.bfloat16)
    text_half = text_units.astype(jnp.bfloat16)
    sigmoid_multiplier = sharpness_coefficient[0]
    bias_value = additive_offset_term[0]
    own_rows = image_half.shape[0]
    own_first = (lax.axis_index("blk") * lax.axis_size("grp") + lax.axis_index("grp")) * own_rows
    text_index = own_first + lax.broadcasted_iota(jnp.int32, (own_rows, 1), 0)
    grads = (jnp.zeros(image_units.shape, jnp.float32), jnp.zeros(text_units.shape, jnp.float32))
    image_block, text_block, owner_ids = (
        lax.all_gather(image_half, "grp", axis=0, tiled=True),
        lax.all_gather(text_half, "grp", axis=0, tiled=True),
        lax.all_gather(matched_caption_ids, "grp", axis=0, tiled=True),
    )
    group_rows = image_block.shape[0]
    cycle_size = lax.axis_size("blk")
    cycle_place = lax.axis_index("blk")
    streams = [(1, 0, (image_block, text_block, owner_ids))]
    for cycle_step in range(cycle_size):
        next_streams = []
        for direction, offset, held_rows in streams:
            anchor = jnp.remainder(cycle_place - direction * cycle_step, cycle_size)
            absorb_text_block = held_rows[1]
            columns = (
                anchor * group_rows
                + offset
                + lax.broadcasted_iota(jnp.int32, (1, absorb_text_block.shape[0]), 1)
            )
            image_labels = (matched_caption_ids[:, None] == columns).astype(jnp.float32)
            text_labels = (text_index == held_rows[2][None, :]).astype(jnp.float32)
            image_part = weighted_sum(
                image_half, absorb_text_block, image_labels, sigmoid_multiplier, bias_value
            )
            text_part = weighted_sum(
                text_half, held_rows[0], text_labels, sigmoid_multiplier, bias_value
            )
            grads = (grads[0] + image_part, grads[1] + text_part)
            if cycle_step + 1 < cycle_size:
                held_rows = pass_on(held_rows, direction)
            next_streams.append((direction, offset, held_rows))
        streams = next_streams
    image_grad = back_through_norm(image_units, image_scale, grads[0])
    text_grad = back_through_norm(text_units, text_scale, grads[1])
    attn_grad = lax.dot_general(
        dense_result_adjoint,
        lax.all_gather(dense_mapping_matrix, "grp", axis=0, tiled=True),
        (((1,), (1,)), ((), ())),
        preferred_element_type=jnp.float32,
    ).astype(jnp.bfloat16)
    weight_share = lax.psum_scatter(
        lax.dot_general(
            heads_mixed_concluding,
            dense_result_adjoint,
            (((0,), (0,)), ((), ())),
            preferred_element_type=jnp.float32,
        ),
        "grp",
        scatter_dimension=0,
        tiled=True,
    )
    weight_total = lax.psum(weight_share, "blk")
    token_count = heads_mixed_concluding.shape[0] * lax.axis_size("blk") * lax.axis_size("grp")
    weight_grad = weight_total * (1.0 / math.sqrt(token_count))
    return (image_grad, text_grad, attn_grad, weight_grad)


def solution(mesh):
    placed = (
        P(("blk", "grp"), None),
        P(("blk", "grp"), None),
        P(("blk", "grp")),
        P(),
        P(),
        P(("blk", "grp"), None),
        P(("blk", "grp"), None),
        P("grp", None),
    )
    return jax.shard_map(
        per_device,
        mesh=mesh,
        in_specs=placed,
        out_specs=(
            P(("blk", "grp"), None),
            P(("blk", "grp"), None),
            P(("blk", "grp"), None),
            P("grp", None),
        ),
        check_vma=False,
    )
```

profile of v0, /device:TPU:0, one launch (start us, length us, event | category | flops | bytes accessed | tf_op | source)
XLA Modules:
  0.0 238.0 jit_solution(2226389386866550796)
XLA Ops:
  7.2 0.0 copy-start
  7.2 0.0 reduce-scatter.2.cloned.1.call-start
  7.2 1.2 copy-done
  8.4 6.6 %fusion.130 = f32[1536,1536]{1,0:T(8,128)} fusion(bf16[384,1536]{1,0:T(8,128)(2,1)} %param.13, bf16[384,1536]{1,0:T(8,128)(2,1)S(1)} %copy-done), kind=kOutput, calls=%fused_computation.161 | convolution fusion | flops 1811939328 | bytes 11796480 | tf_op jit(solution)/shard_map/dot_general | solution.py:112
  15.0 0.0 reduce-scatter.2.cloned.1.call-update
  15.0 0.0 all-gather.2.cloned.1.call-start
  15.1 0.7 all-gather.2.cloned.1.call-update
  15.8 0.0 all-reduce.3.cloned.1.call-start
  15.8 0.0 copy-done.2
  15.9 0.1 multiply_reduce_fusion.3
  16.0 0.1 multiply_convert_fusion.1
  16.1 16.5 %all_gather.13 = bf16[128,1152]{1,0:T(8,128)(2,1)S(1)} all-gather(bf16[16,1152]{1,0:T(8,128)(2,1)S(1)} %multiply_convert_fusion.1), channel_id=1, replica_groups=mesh['blk'=4,'grp'=8] {'grp'}, dimensions={0}, use_global_device_ids=true | all-gather | bytes 331776 | tf_op jit(solution)/shard_map/all_gather | solution.py:72
  32.6 1.5 collective-permute-start.3
  34.2 0.6 dynamic-slice
  35.4 0.2 dynamic-update-slice
  35.7 9.6 %all-reduce = s32[128]{0:T(128)S(1)} all-reduce(s32[128]{0:T(128)S(1)} %dynamic-update-slice), channel_id=1, replica_groups=mesh['blk'=4,'grp'=8] {'grp'}, use_global_device_ids=true, to_apply=%add | all-reduce | flops 128 | bytes 1024
  45.3 1.5 collective-permute-start.4
  46.8 0.1 multiply_reduce_fusion.2
  46.9 0.1 multiply_convert_fusion
  47.0 15.9 %all_gather.12 = bf16[128,1152]{1,0:T(8,128)(2,1)S(1)} all-gather(bf16[16,1152]{1,0:T(8,128)(2,1)S(1)} %multiply_convert_fusion), channel_id=1, replica_groups=mesh['blk'=4,'grp'=8] {'grp'}, dimensions={0}, use_global_device_ids=true | all-gather | bytes 331776 | tf_op jit(solution)/shard_map/all_gather | solution.py:73
  62.9 1.5 collective-permute-start
  65.8 0.4 fusion.64
  66.2 0.5 fusion.65
  66.7 0.0 collective-permute-done.4
  66.7 0.3 collective-permute-start.6
  67.0 6.1 %collective-permute-done.6 = s32[128]{0:T(128)S(1)} collective-permute-done((s32[128]{0:T(128)S(1)}, s32[128]{0:T(128)S(1)}, u32[]{:S(2)}, u32[]{:S(2)}) %collective-permute-start.6) | collective-permute-done | bytes 544 | tf_op jit(solution)/shard_map/ppermute | solution.py:21
  73.1 0.6 collective-permute-start.8
  73.7 1.2 collective-permute-start.5
  74.9 0.8 collective-permute-start.1
  75.7 0.4 convolution_add_fusion.2
  76.2 0.5 convolution_add_fusion.5
  76.6 8.0 %collective-permute-done.5 = bf16[128,1152]{1,0:T(8,128)(2,1)S(1)} collective-permute-done((bf16[128,1152]{1,0:T(8,128)(2,1)S(1)}, bf16[128,1152]{1,0:T(8,128)(2,1)S(1)}, u32[]{:S(2)}, u32[]{:S(2)}) %collective-permute-start.5) | collective-permute-done | bytes 294944 | tf_op jit(solution)/shard_map/ppermute | solution.py:21
  84.6 0.3 collective-permute-start.7
  84.9 6.0 %collective-permute-done.1 = bf16[128,1152]{1,0:T(8,128)(2,1)S(1)} collective-permute-done((bf16[128,1152]{1,0:T(8,128)(2,1)S(1)}, bf16[128,1152]{1,0:T(8,128)(2,1)S(1)}, u32[]{:S(2)}, u32[]{:S(2)}) %collective-permute-start.1) | collective-permute-done | bytes 294944 | tf_op jit(solution)/shard_map/ppermute | solution.py:21
  90.9 0.3 collective-permute-start.2
  91.2 0.4 convolution_add_fusion.1
  91.6 0.5 convolution_add_fusion.4
  92.1 5.1 %collective-permute-done.7 = bf16[128,1152]{1,0:T(8,128)(2,1)S(1)} collective-permute-done((bf16[128,1152]{1,0:T(8,128)(2,1)S(1)}, bf16[128,1152]{1,0:T(8,128)(2,1)S(1)}, u32[]{:S(2)}, u32[]{:S(2)}) %collective-permute-start.7) | collective-permute-done | bytes 294944 | tf_op jit(solution)/shard_map/ppermute | solution.py:21
  97.2 0.6 multiply_reduce_fusion
  97.8 0.7 subtract_multiply_fusion
  98.5 22.6 %reduce-scatter.2.cloned.1.call-done = f32[192,1536]{1,0:T(8,128)} async-done(((f32[1536,1536]{1,0:T(8,128)}), f32[192,1536]{1,0:T(8,128)}) %reduce-scatter.2.cloned.1.call-update) | async-done | bytes 1179664 | tf_op jit(solution)/shard_map/reduce_scatter | solution.py:111
  121.2 0.0 all-reduce.3.cloned.1.call-update
  121.2 0.6 multiply_reduce_fusion.1
  121.8 0.7 subtract_multiply_fusion.1
  122.5 50.2 %all-gather.2.cloned.1.call-done = bf16[1536,1536]{1,0:T(8,128)(2,1)} async-done(((bf16[192,1536]{1,0:T(8,128)(2,1)}), bf16[1536,1536]{1,0:T(8,128)(2,1)}) %all-gather.2.cloned.1.call-update) | async-done | bytes 4718608 | tf_op jit(solution)/shard_map/all_gather | solution.py:107
  172.7 5.4 %convolution_convert_fusion = bf16[384,1536]{1,0:T(8,128)(2,1)} fusion(bf16[384,1536]{1,0:T(8,128)(2,1)S(1)} %copy-done, bf16[1536,1536]{1,0:T(8,128)(2,1)} %all-gather.2.cloned.1.call-done), kind=kOutput, calls=%fused_computation | convolution fusion | flops 1812529152 | bytes 7077888 | tf_op jit(solution)/shard_map/dot_general | solution.py:105
  178.0 51.1 %all-reduce.3.cloned.1.call-done = f32[192,1536]{1,0:T(8,128)} async-done(((f32[192,1536]{1,0:T(8,128)}), f32[192,1536]{1,0:T(8,128)}) %all-reduce.3.cloned.1.call-update) | async-done | bytes 1179664 | tf_op jit(solution)/shard_map/psum | solution.py:122
  229.1 2.4 %broadcast_multiply_fusion = f32[192,1536]{1,0:T(8,128)} fusion(f32[192,1536]{1,0:T(8,128)} %all-reduce.3.cloned.1.call-done), kind=kLoop, calls=%fused_computation.81 | loop fusion | flops 294912 | bytes 2359296 | tf_op jit(solution)/shard_map/mul | solution.py:124
  (19 shorter events, 0.1 us)
Async XLA Ops:
  7.2 1.3 copy-start
  7.2 114.0 %reduce-scatter.2.cloned.1.call-start = ((), (), s32[]{:S(2)}) async-start(), calls=%async_computation.2 | async-start | bytes 10616832 | tf_op jit(solution)/shard_map/reduce_scatter | solution.py:111
  15.0 0.9 copy-start.2
  15.0 19.2 %copy-start.4 = (u32[32]{0:T(128)S(1)}, u32[32]{0:T(128)}, u32[]{:S(2)}) copy-start(u32[32]{0:T(128)} %constant.61) | copy-start | bytes 388
  15.0 20.4 %copy-start.3 = (s32[16]{0:T(128)S(1)}, s32[16]{0:T(128)}, u32[]{:S(2)}) copy-start(s32[16]{0:T(128)} %param.10) | copy-start | bytes 196
  15.0 31.8 %copy-start.1 = (f32[16,1152]{1,0:T(8,128)S(1)}, f32[16,1152]{1,0:T(8,128)}, u32[]{:S(2)}) copy-start(f32[16,1152]{1,0:T(8,128)} %param.9) | copy-start | bytes 221188
  15.0 157.6 %all-gather.2.cloned.1.call-start = ((), (), s32[]{:S(2)}) async-start(), calls=%async_computation.1 | async-start | bytes 5308416 | tf_op jit(solution)/shard_map/all_gather | solution.py:107
  15.8 213.3 %all-reduce.3.cloned.1.call-start = ((), (), s32[]{:S(2)}) async-start(), calls=%async_computation.3 | async-start | bytes 2359296 | tf_op jit(solution)/shard_map/psum | solution.py:122
  32.6 41.1 %collective-permute-start.3 = (bf16[128,1152]{1,0:T(8,128)(2,1)S(1)}, bf16[128,1152]{1,0:T(8,128)(2,1)S(1)}, u32[]{:S(2)}, u32[]{:S(2)}) collective-permute-start(bf16[128,1152]{1,0:T(8,128)(2,1)S(1)} %all_gather.13), channel_id=1, source_target_pairs={{0,8},{8,16},{16,24},{24,0},{1,9},{9,17},{17,25},{25,1},{2,10},{10... | collective-permute-start | bytes 884744 | tf_op jit(solution)/shard_map/ppermute | solution.py:21
  45.3 21.4 %collective-permute-start.4 = (s32[128]{0:T(128)S(1)}, s32[128]{0:T(128)S(1)}, u32[]{:S(2)}, u32[]{:S(2)}) collective-permute-start(s32[128]{0:T(128)S(1)} %all-reduce), channel_id=1, source_target_pairs={{0,8},{8,16},{16,24},{24,0},{1,9},{9,17},{17,25},{25,1},{2,10},{10... | collective-permute-start | bytes 1544 | tf_op jit(solution)/shard_map/ppermute | solution.py:21
  62.9 12.0 %collective-permute-start = (bf16[128,1152]{1,0:T(8,128)(2,1)S(1)}, bf16[128,1152]{1,0:T(8,128)(2,1)S(1)}, u32[]{:S(2)}, u32[]{:S(2)}) collective-permute-start(bf16[128,1152]{1,0:T(8,128)(2,1)S(1)} %all_gather.12), channel_id=1, source_target_pairs={{0,8},{8,16},{16,24},{24,0},{1,9},{9,17},{17,25},{25,1},{2,10},{10... | collective-permute-start | bytes 884744 | tf_op jit(solution)/shard_map/ppermute | solution.py:21
  66.7 6.5 %collective-permute-start.6 = (s32[128]{0:T(128)S(1)}, s32[128]{0:T(128)S(1)}, u32[]{:S(2)}, u32[]{:S(2)}) collective-permute-start(s32[128]{0:T(128)S(1)} %collective-permute-done.4), channel_id=1, source_target_pairs={{0,8},{8,16},{16,24},{24,0},{1,9},{9,17},{17,25},{25,1},{2,10},{10... | collective-permute-start | bytes 1544 | tf_op jit(solution)/shard_map/ppermute | solution.py:21
  73.1 18.9 %collective-permute-start.8 = (s32[128]{0:T(128)S(1)}, s32[128]{0:T(128)S(1)}, u32[]{:S(2)}, u32[]{:S(2)}) collective-permute-start(s32[128]{0:T(128)S(1)} %collective-permute-done.6), channel_id=1, source_target_pairs={{0,8},{8,16},{16,24},{24,0},{1,9},{9,17},{17,25},{25,1},{2,10},{10... | collective-permute-start | bytes 1544 | tf_op jit(solution)/shard_map/ppermute | solution.py:21
  73.7 10.8 %collective-permute-start.5 = (bf16[128,1152]{1,0:T(8,128)(2,1)S(1)}, bf16[128,1152]{1,0:T(8,128)(2,1)S(1)}, u32[]{:S(2)}, u32[]{:S(2)}) collective-permute-start(bf16[128,1152]{1,0:T(8,128)(2,1)S(1)} %collective-permute-done.3), channel_id=1, source_target_pairs={{0,8},{8,16},{16,24},{24,0},{1,9},{9,17},{17,25},{25,1},{2,10},{10... | collective-permute-start | bytes 884744 | tf_op jit(solution)/shard_map/ppermute | solution.py:21
  74.9 16.0 %collective-permute-start.1 = (bf16[128,1152]{1,0:T(8,128)(2,1)S(1)}, bf16[128,1152]{1,0:T(8,128)(2,1)S(1)}, u32[]{:S(2)}, u32[]{:S(2)}) collective-permute-start(bf16[128,1152]{1,0:T(8,128)(2,1)S(1)} %collective-permute-done), channel_id=1, source_target_pairs={{0,8},{8,16},{16,24},{24,0},{1,9},{9,17},{17,25},{25,1},{2,10},{10... | collective-permute-start | bytes 884744 | tf_op jit(solution)/shard_map/ppermute | solution.py:21
  84.6 12.6 %collective-permute-start.7 = (bf16[128,1152]{1,0:T(8,128)(2,1)S(1)}, bf16[128,1152]{1,0:T(8,128)(2,1)S(1)}, u32[]{:S(2)}, u32[]{:S(2)}) collective-permute-start(bf16[128,1152]{1,0:T(8,128)(2,1)S(1)} %collective-permute-done.5), channel_id=1, source_target_pairs={{0,8},{8,16},{16,24},{24,0},{1,9},{9,17},{17,25},{25,1},{2,10},{10... | collective-permute-start | bytes 884744 | tf_op jit(solution)/shard_map/ppermute | solution.py:21
  90.9 30.3 %collective-permute-start.2 = (bf16[128,1152]{1,0:T(8,128)(2,1)S(1)}, bf16[128,1152]{1,0:T(8,128)(2,1)S(1)}, u32[]{:S(2)}, u32[]{:S(2)}) collective-permute-start(bf16[128,1152]{1,0:T(8,128)(2,1)S(1)} %collective-permute-done.1), channel_id=1, source_target_pairs={{0,8},{8,16},{16,24},{24,0},{1,9},{9,17},{17,25},{25,1},{2,10},{10... | collective-permute-start | bytes 884744 | tf_op jit(solution)/shard_map/ppermute | solution.py:21
Sparse Core Ops, SparseCore 0:
  15.2 105.9 reduce-scatter.1
  122.8 49.8 all-gather.1
  175.8 53.2 all-reduce.2
where the time goes:
time: 238 us
  waiting for transfers between devices  150 us (63%)
  blocking collectives  42.1 us (18%)
  between operations  15.8 us (7%)
  matrix products  15.7 us (7%)
  starting transfers between devices  8.08 us (3%)
  other arithmetic  4.29 us (2%)
    psum x1, waiting for transfers between devices, per_device(): weight_total = lax.psum(weight_share, 'blk')  51.1 us
    all_gather x1, waiting for transfers between devices, per_device(): lax.all_gather(dense_mapping_matrix, 'grp', axis=0, tiled=True)  50.2 us
    ppermute x9, waiting for transfers between devices, passed_along(): return lax.ppermute(x, axis, [(i, (i + by) % peers) for i in range(peers)])  25.3 us
    reduce_scatter x1, waiting for transfers between devices, per_device(): lax.psum_scatter(lax.dot_general(heads_mixed_concluding, dense_result_adj...  22.6 us
    all_gather x1, blocking collectives, per_device(): lax.all_gather(image_half, 'grp', axis=0, tiled=True)  16.5 us
    all_gather x1, blocking collectives, per_device(): lax.all_gather(text_half, 'grp', axis=0, tiled=True)  15.9 us
    unnamed x1, blocking collectives  9.65 us
    ppermute x9, starting transfers between devices, passed_along(): return lax.ppermute(x, axis, [(i, (i + by) % peers) for i in range(peers)])  7.97 us
  transfers between devices with their start and end apart: 12, of which 7 were waited for; matrix products, arithmetic and copies ran while one was open for 5% of the time, Pallas kernels for 0%

commit v1 on v0

--- a/solution.py
+++ b/solution.py
@@ -1,8 +1,11 @@
+import functools
 import math
 
 import jax
 import jax.numpy as jnp
 from jax import lax
+from jax.experimental import pallas as pl
+from jax.experimental.pallas import tpu as pltpu
 from jax.sharding import PartitionSpec as P
 
 stability_floor = 1e-06
@@ -48,7 +51,7 @@
     )
 
 
-def per_device(
+def plain_device(
     picture_vectors_prenorm,
     caption_vectors_prenorm,
     matched_caption_ids,
@@ -125,6 +128,403 @@
     return (image_grad, text_grad, attn_grad, weight_grad)
 
 
+MESH = pl.DeviceIdType.MESH
+f32 = jnp.float32
+bf16 = jnp.bfloat16
+
+
+def fused_kernel(
+    blks,
+    zs,
+    scale,
+    sharp_ref,
+    bias_ref,
+    ids_ref,
+    pic_hbm,
+    cap_hbm,
+    heads_hbm,
+    adj_hbm,
+    w_hbm,
+    pic_out,
+    cap_out,
+    attn_out,
+    wgrad_out,
+    pic_ref,
+    cap_ref,
+    heads_ref,
+    adj_ref,
+    heads_t,
+    heads_peer,
+    adj_peer,
+    w_full,
+    part,
+    first_in,
+    second,
+    second_in,
+    zsum,
+    zsum_in,
+    done,
+    img,
+    img_ids,
+    txt,
+    img_part,
+    img_core_in,
+    img_z,
+    img_z_in,
+    txt_part,
+    txt_in,
+    load_sem,
+    core_sem,
+    wz_sem,
+    w1_sem,
+    w2_sem,
+    wc_sem,
+    first_sem,
+    second_sem,
+    zsum_sem,
+    done_sem,
+    iz_sem,
+    tb_sem,
+    ir_sem,
+    tr_sem,
+):
+    b = lax.axis_index("blk")
+    g = lax.axis_index("grp")
+    z = g // 2
+    c = g % 2
+    rows, cols = w_hbm.shape
+    chunk = rows // blks
+    wide = 2 * rows
+    own, width = pic_ref.shape
+    flip = {1: b + 1 - 2 * lax.rem(b, 2), 2: lax.rem(b + 2, 4)}
+    flip[3] = flip[1] + flip[2] - b
+
+    def blk_peer(d):
+        return (lax.rem(b + d, blks), g)
+
+    def z_of(d):
+        return lax.rem(z + zs + d, zs)
+
+    def z_peer(d):
+        return (b, z_of(d) * 2 + c)
+
+    def rows_of(i):
+        return pl.ds(pl.multiple_of(i * chunk, 16), chunk)
+
+    partner = (b, z * 2 + 1 - c)
+    mine = rows_of(b)
+
+    def rcopy(src, dst, sems, to):
+        return pltpu.make_async_remote_copy(
+            src_ref=src, dst_ref=dst, send_sem=sems.at[0], recv_sem=sems.at[1],
+            device_id=to, device_id_type=MESH,
+        )
+
+    sent = []
+
+    def go(src, dst, sems, to):
+        copy = rcopy(src, dst, sems, to)
+        copy.start()
+        sent.append(copy)
+
+    def arrived(dst, sems):
+        rcopy(dst, dst, sems, partner).wait_recv()
+
+    barrier = pltpu.get_barrier_semaphore()
+    peers = [blk_peer(d) for d in range(1, blks)] + [z_peer(d) for d in range(1, zs)] + [partner]
+    for peer in peers:
+        pl.semaphore_signal(barrier, inc=1, device_id=peer, device_id_type=MESH)
+    loads = [
+        pltpu.make_async_copy(src, dst, load_sem.at[i])
+        for i, (src, dst) in enumerate(
+            [
+                (heads_hbm, heads_ref),
+                (pic_hbm, pic_ref),
+                (cap_hbm, cap_ref),
+                (adj_hbm, adj_ref),
+                (w_hbm, w_full.at[z, c]),
+            ]
+        )
+    ]
+    for load in loads:
+        load.start()
+    place = lax.broadcasted_iota(jnp.int32, (own, 128), 0)
+    tile_ids = jnp.zeros((own, 128), jnp.int32)
+    for i in range(own):
+        tile_ids = jnp.where(place == i, ids_ref[i], tile_ids)
+    img_ids[c, z] = tile_ids
+
+    pl.semaphore_wait(barrier, len(peers))
+    go(adj_hbm, adj_peer, core_sem.at[0], partner)
+    for d in range(1, zs):
+        go(w_hbm.at[mine], w_full.at[z, c, mine], wz_sem.at[d - 1], z_peer(d))
+
+    loads[0].wait()
+    for t in range(zs):
+        turned = heads_ref[:, t * wide:(t + 1) * wide].T
+        heads_t[0, t] = turned[:rows]
+        heads_t[1, t] = turned[rows:]
+    go(heads_t.at[1 - c], heads_peer, core_sem.at[1], partner)
+
+    loads[1].wait()
+    loads[2].wait()
+    image_units, image_scale = unit_rows(pic_ref[...])
+    text_units, text_scale = unit_rows(cap_ref[...])
+    img[c, z] = image_units.astype(bf16)
+    txt[b] = text_units.astype(bf16)
+    for d in range(1, zs):
+        go(img.at[c, z], img.at[c, z], iz_sem.at[d - 1, 0], z_peer(d))
+        go(img_ids.at[c, z], img_ids.at[c, z], iz_sem.at[d - 1, 1], z_peer(d))
+    for d in range(1, blks):
+        go(txt.at[b], txt.at[b], tb_sem.at[d - 1], blk_peer(d))
+    go(w_hbm, w_full.at[z, c], wc_sem.at[0], partner)
+
+    loads[3].wait()
+    arrived(adj_peer, core_sem.at[0])
+    arrived(heads_peer, core_sem.at[1])
+    tile = cols // 3 if cols % 384 == 0 else cols
+    for k in range(zs):
+        t = z_of(k + 1)
+        for j in range(0, cols, tile):
+            part[k, :, j:j + tile] = (
+                jnp.dot(heads_t[c, t], adj_ref[:, j:j + tile], preferred_element_type=f32)
+                + jnp.dot(heads_peer[t], adj_peer[:, j:j + tile], preferred_element_type=f32)
+            ).astype(bf16)
+        f = 1 + k % 2
+        to = (flip[f], g)
+        go(part.at[k, rows_of(flip[3])], first_in.at[k, 1], first_sem.at[k, 1], to)
+        go(part.at[k, rows_of(flip[f])], first_in.at[k, 0], first_sem.at[k, 0], to)
+
+    for d in range(1, zs):
+        arrived(img.at[c, z_of(-d)], iz_sem.at[d - 1, 0])
+        arrived(img_ids.at[c, z_of(-d)], iz_sem.at[d - 1, 1])
+    go(img.at[c], img.at[c], core_sem.at[2], partner)
+    go(img_ids.at[c], img_ids.at[c], core_sem.at[3], partner)
+
+    half = cols // 2
+
+    def w_piece(e, i, h):
+        return w_full.at[z_of(-e), c, rows_of(i), h * half:(h + 1) * half]
+
+    def w_first(e):
+        arrived(w_full.at[z_of(-e), c, mine], wz_sem.at[e - 1])
+        for h in range(2):
+            piece = w_piece(e, b, h)
+            go(piece, piece, w1_sem.at[e - 1, h], (flip[1 + h], g))
+
+    def w_second(e):
+        for h in range(2):
+            got = w_piece(e, flip[1 + h], h)
+            arrived(got, w1_sem.at[e - 1, h])
+            to = (flip[2 - h], g)
+            go(got, got, w2_sem.at[e - 1, h, 0], to)
+            piece = w_piece(e, b, h)
+            go(piece, piece, w2_sem.at[e - 1, h, 1], to)
+
+    def w_core(e):
+        for h in range(2):
+            arrived(w_piece(e, flip[3], h), w2_sem.at[e - 1, h, 0])
+            arrived(w_piece(e, flip[2 - h], h), w2_sem.at[e - 1, h, 1])
+        block = w_full.at[z_of(-e), c]
+        go(block, block, wc_sem.at[e], partner)
+
+    def own_attn(e):
+        zf = z_of(-e)
+        arrived(w_full.at[zf, 1 - c], wc_sem.at[e])
+        both = w_full[zf].reshape(wide, cols)
+        attn_out[:, pl.ds(pl.multiple_of(zf * wide, 128), wide)] = lax.dot_general(
+            adj_ref[...], both, (((1,), (1,)), ((), ())), preferred_element_type=f32
+        ).astype(bf16)
+
+    def step_two(k):
+        s = 2 - k % 2
+        arrived(first_in.at[k, 1], first_sem.at[k, 1])
+        second[k] = (
+            part[k, rows_of(flip[s])].astype(f32) + first_in[k, 1].astype(f32)
+        ).astype(bf16)
+        go(second.at[k], second_in.at[k], second_sem.at[k], (flip[s], g))
+
+    def step_three(k):
+        arrived(first_in.at[k, 0], first_sem.at[k, 0])
+        arrived(second_in.at[k], second_sem.at[k])
+        total = (
+            part[k, mine].astype(f32) + first_in[k, 0].astype(f32) + second_in[k].astype(f32)
+        )
+        if k < zs - 1:
+            zsum[k] = total.astype(bf16)
+            go(zsum.at[k], zsum_in.at[k], zsum_sem.at[k], z_peer(k + 1))
+        return total
+
+    loads[4].wait()
+    own_attn(0)
+
+    for d in range(1, blks):
+        arrived(txt.at[lax.rem(b + blks - d, blks)], tb_sem.at[d - 1])
+    arrived(img.at[1 - c], core_sem.at[2])
+    arrived(img_ids.at[1 - c], core_sem.at[3])
+    image_rows = 2 * zs * own
+    text_rows = blks * own
+    images = img[...].reshape(image_rows, width)
+    texts = txt[...].reshape(text_rows, width)
+    owners = img_ids[...].reshape(image_rows, 128)[:, :1]
+    lane = lax.broadcasted_iota(jnp.int32, (image_rows, text_rows), 1)
+    column = ((lane // own) * (2 * zs) + g) * own + lane % own
+    labels = (owners == column).astype(f32)
+    inner_dots = lax.dot_general(
+        images, texts, (((1,), (1,)), ((), ())), preferred_element_type=f32
+    )
+    sharp = sharp_ref[0]
+    pair = sharp * (jax.nn.sigmoid(sharp * inner_dots + bias_ref[0]) - labels)
+    img_part[...] = jnp.dot(pair.astype(bf16), texts, preferred_element_type=f32).reshape(
+        2, zs, own, width
+    )
+    txt_part[...] = jnp.dot(
+        pair.T.astype(bf16), images, preferred_element_type=f32
+    ).reshape(blks, own, width)
+    go(img_part.at[1 - c], img_core_in, core_sem.at[4], partner)
+    for d in range(1, blks):
+        to = blk_peer(d)
+        go(txt_part.at[to[0]], txt_in.at[d - 1], tr_sem.at[d - 1], to)
+
+    w_first(1)
+    step_two(0)
+    step_two(1)
+    for e in range(2, zs):
+        w_first(e)
+        step_two(e)
+    arrived(img_core_in, core_sem.at[4])
+    img_z[...] = img_part[c] + img_core_in[...]
+    for d in range(1, zs):
+        go(img_z.at[z_of(d)], img_z_in.at[d - 1], ir_sem.at[d - 1], z_peer(d))
+    for k in range(zs):
+        total = step_three(k)
+        if 1 <= k:
+            w_second(k)
+
+    for k in range(zs - 1):
+        arrived(zsum_in.at[k], zsum_sem.at[k])
+        total += zsum_in[k].astype(f32)
+    done[0] = (total * scale).astype(bf16)
+    for d in range(1, blks):
+        go(done.at[0], done.at[d], done_sem.at[d - 1], blk_peer(d))
+
+    for e in range(1, zs):
+        w_core(e)
+        if e > 1:
+            own_attn(e - 1)
+
+    image_grad = img_z[z]
+    for d in range(1, zs):
+        arrived(img_z_in.at[d - 1], ir_sem.at[d - 1])
+        image_grad += img_z_in[d - 1]
+    pic_out[...] = back_through_norm(image_units, image_scale, image_grad)
+    text_grad = txt_part[b]
+    for d in range(1, blks):
+        arrived(txt_in.at[d - 1], tr_sem.at[d - 1])
+        text_grad += txt_in[d - 1]
+    cap_out[...] = back_through_norm(text_units, text_scale, text_grad)
+
+    own_attn(zs - 1)
+    wgrad_out[mine] = done[0].astype(f32)
+    for d in range(1, blks):
+        arrived(done.at[d], done_sem.at[d - 1])
+        wgrad_out[rows_of(lax.rem(b + blks - d, blks))] = done[d].astype(f32)
+
+    for copy in sent:
+        copy.wait_send()
+
+
+def fused_device(blks, grps, pic, cap, ids, sharp, bias, heads, adj, w):
+    zs = grps // 2
+    own, width = pic.shape
+    tokens, cols = adj.shape
+    rows = w.shape[0]
+    chunk = rows // blks
+    scale = 1.0 / math.sqrt(tokens * blks * grps)
+    vmem = pl.BlockSpec(memory_space=pltpu.VMEM)
+    smem = pl.BlockSpec(memory_space=pltpu.SMEM)
+    hbm = pl.BlockSpec(memory_space=pl.ANY)
+    dma = pltpu.SemaphoreType.DMA
+    return pl.pallas_call(
+        functools.partial(fused_kernel, blks, zs, scale),
+        out_shape=(
+            jax.ShapeDtypeStruct(pic.shape, f32),
+            jax.ShapeDtypeStruct(cap.shape, f32),
+            jax.ShapeDtypeStruct(heads.shape, bf16),
+            jax.ShapeDtypeStruct(w.shape, f32),
+        ),
+        in_specs=[smem] * 3 + [hbm] * 5,
+        out_specs=(vmem,) * 4,
+        scratch_shapes=[
+            pltpu.VMEM(pic.shape, f32),
+            pltpu.VMEM(cap.shape, f32),
+            pltpu.VMEM((tokens, cols), bf16),
+            pltpu.VMEM((tokens, cols), bf16),
+            pltpu.VMEM((2, zs, rows, tokens), bf16),
+            pltpu.VMEM((zs, rows, tokens), bf16),
+            pltpu.VMEM((tokens, cols), bf16),
+            pltpu.VMEM((zs, 2, rows, cols), bf16),
+            pltpu.VMEM((zs, rows, cols), bf16),
+            pltpu.VMEM((zs, 2, chunk, cols), bf16),
+            pltpu.VMEM((zs, chunk, cols), bf16),
+            pltpu.VMEM((zs, chunk, cols), bf16),
+            pltpu.VMEM((zs - 1, chunk, cols), bf16),
+            pltpu.VMEM((zs - 1, chunk, cols), bf16),
+            pltpu.VMEM((blks, chunk, cols), bf16),
+            pltpu.VMEM((2, zs, own, width), bf16),
+            pltpu.VMEM((2, zs, own, 128), jnp.int32),
+            pltpu.VMEM((blks, own, width), bf16),
+            pltpu.VMEM((2, zs, own, width), f32),
+            pltpu.VMEM((zs, own, width), f32),
+            pltpu.VMEM((zs, own, width), f32),
+            pltpu.VMEM((zs - 1, own, width), f32),
+            pltpu.VMEM((blks, own, width), f32),
+            pltpu.VMEM((blks - 1, own, width), f32),
+            dma((5,)),
+            dma((5, 2)),
+            dma((zs - 1, 2)),
+            dma((zs - 1, 2, 2)),
+            dma((zs - 1, 2, 2, 2)),
+            dma((zs, 2)),
+            dma((zs, 2, 2)),
+            dma((zs, 2)),
+            dma((zs - 1, 2)),
+            dma((blks - 1, 2)),
+            dma((zs - 1, 2, 2)),
+            dma((blks - 1, 2)),
+            dma((zs - 1, 2)),
+            dma((blks - 1, 2)),
+        ],
+        compiler_params=pltpu.CompilerParams(
+            collective_id=0, has_side_effects=True, vmem_limit_bytes=56 * 1024 * 1024
+        ),
+        cost_estimate=pl.CostEstimate(
+            flops=4 * tokens * cols * cols, bytes_accessed=8 * tokens * cols, transcendentals=0
+        ),
+    )(sharp, bias, ids, pic, cap, heads, adj, w)
+
+
+def per_device(pic, cap, ids, sharp, bias, heads, adj, w):
+    blks = lax.axis_size("blk")
+    grps = lax.axis_size("grp")
+    own = pic.shape[0]
+    rows, cols = w.shape
+    fits = (
+        grps % 2 == 0
+        and grps >= 4
+        and blks == 4
+        and rows % (16 * blks) == 0
+        and (2 * rows) % 128 == 0
+        and heads.shape[1] == rows * grps
+        and cols == heads.shape[1]
+        and own % 16 == 0
+        and cols % 256 == 0
+    )
+    if not fits:
+        return plain_device(pic, cap, ids, sharp, bias, heads, adj, w)
+    return fused_device(blks, grps, pic, cap, ids, sharp, bias, heads, adj, w)
+
+
 def solution(mesh):
     placed = (
         P(("blk", "grp"), None),

time: 238 us -> 69 us (0.29)
  waiting for transfers between devices: 150 us -> 0 us
  Pallas kernels: 0 us -> 60.3 us
  blocking collectives: 42.1 us -> 0 us
  matrix products: 15.7 us -> 0 us
  between operations: 15.8 us -> 1.93 us
  starting transfers between devices: 8.08 us -> 0 us
  local copies, waits for them, and re-layouts: 2.11 us -> 6.51 us
  other arithmetic: 4.29 us -> 0 us
    pallas_call x0 -> x1, Pallas kernels: none -> 60.3 us  [fused_device(): pl.pallas_call(functools.partial(fused_kernel, blks, zs, scale), out_shap...]
    psum x1 -> x0, waiting for transfers between devices: 51.1 us -> none  [per_device(): weight_total = lax.psum(weight_share, 'blk')]
    all_gather x1 -> x0, waiting for transfers between devices: 50.2 us -> none  [per_device(): lax.all_gather(dense_mapping_matrix, 'grp', axis=0, tiled=True)]
    all_gather x2 -> x0, blocking collectives: 32.5 us -> none  [the longest x1 16.5 us: per_device(): lax.all_gather(image_half, 'grp', axis=0, tiled=True)]
    ppermute x9 -> x0, waiting for transfers between devices: 25.3 us -> none  [passed_along(): return lax.ppermute(x, axis, [(i, (i + by) % peers) for i in range(peers)])]
    reduce_scatter x1 -> x0, waiting for transfers between devices: 22.6 us -> none  [per_device(): lax.psum_scatter(lax.dot_general(heads_mixed_concluding, dense_result_adj...]
    dot_general x10 -> x0, matrix products: 15.7 us -> none  [the longest x1 6.56 us: per_device(): lax.dot_general(heads_mixed_concluding, dense_result_adjoint, (((0,), (0,...]
    unnamed x1 -> x0, blocking collectives: 9.65 us -> none
  transfers between devices with their start and end apart: 12 -> 0, of which waited for: 7 -> 0; matrix products, arithmetic and copies ran while one was open for 5% -> 0% of each run, Pallas kernels for 0% -> 0%
where the time goes in v1:
time: 69 us; the launch traced here: 68.7 us
  Pallas kernels  60.3 us (87%)
  local copies, waits for them, and re-layouts  6.51 us (9%)
  between operations  1.93 us (3%)
    pallas_call x1, Pallas kernels, fused_device(): pl.pallas_call(functools.partial(fused_kernel, blks, zs, scale), out_shap...  60.3 us
    unnamed x6, local copies, waits for them, and re-layouts  6.51 us

profile of v1, /device:TPU:0, one launch (start us, length us, event | category | flops | bytes accessed | tf_op | source)
XLA Modules:
  0.0 68.7 jit_solution(17936243259548762437)
XLA Ops:
  1.9 60.3 %shard_map.111 = (f32[16,1152]{1,0:T(8,128)}, f32[16,1152]{1,0:T(8,128)}, bf16[384,1536]{1,0:T(8,128)(2,1)}, f32[192,1536]{1,0:T(8,128)}) custom-call(f32[1]{0:T(128)S(6)} %copy.16.sharp_ref, f32[1]{0:T(128)S(6)} %copy.17.bias_ref, s32[16]{0:T(128)} %ids_ref.1, f32[16,1152]{1,0:T(8,128)} %pic_hbm.1, f32[16,1152]{1,0:T(8,128)} %cap_hbm.1, ...), custom_call_target="tpu_custom_call" | custom-call | flops 3623878656 | bytes 4718592 | tf_op jit(solution)/shard_map/pallas_call | solution.py:448
  62.2 1.5 %copy.18 = f32[16,1152]{1,0:T(8,128)} copy(f32[16,1152]{1,0:T(8,128)} %get-tuple-element.8) | data formatting | bytes 147456
  63.7 1.5 %copy.19 = f32[16,1152]{1,0:T(8,128)} copy(f32[16,1152]{1,0:T(8,128)} %get-tuple-element.9) | data formatting | bytes 147456
  65.2 0.0 copy-start
  65.2 2.5 %copy.20 = bf16[384,1536]{1,0:T(8,128)(2,1)} copy(bf16[384,1536]{1,0:T(8,128)(2,1)} %get-tuple-element.10) | data formatting | bytes 2359296
  67.7 0.0 copy-done
  67.7 1.0 %copy.21 = f32[192,1536]{1,0:T(8,128)} copy(f32[192,1536]{1,0:T(8,128)S(1)} %copy-done) | data formatting | bytes 2359296
Async XLA Ops:
  65.2 2.5 %copy-start = (f32[192,1536]{1,0:T(8,128)S(1)}, f32[192,1536]{1,0:T(8,128)}, u32[]{:S(2)}) copy-start(f32[192,1536]{1,0:T(8,128)} %get-tuple-element.11) | copy-start | bytes 3538948

commit v2 on v1

--- a/solution.py
+++ b/solution.py
@@ -238,9 +238,9 @@
         pltpu.make_async_copy(src, dst, load_sem.at[i])
         for i, (src, dst) in enumerate(
             [
-                (heads_hbm, heads_ref),
                 (pic_hbm, pic_ref),
                 (cap_hbm, cap_ref),
+                (heads_hbm, heads_ref),
                 (adj_hbm, adj_ref),
                 (w_hbm, w_full.at[z, c]),
             ]
@@ -253,55 +253,54 @@
     for i in range(own):
         tile_ids = jnp.where(place == i, ids_ref[i], tile_ids)
     img_ids[c, z] = tile_ids
+    loads[0].wait()
+    loads[1].wait()
+    image_units, image_scale = unit_rows(pic_ref[...])
+    text_units, text_scale = unit_rows(cap_ref[...])
+    img[c, z] = image_units.astype(bf16)
+    txt[b] = text_units.astype(bf16)
 
     pl.semaphore_wait(barrier, len(peers))
     go(adj_hbm, adj_peer, core_sem.at[0], partner)
     for d in range(1, zs):
+        go(img.at[c, z], img.at[c, z], iz_sem.at[d - 1, 0], z_peer(d))
+        go(img_ids.at[c, z], img_ids.at[c, z], iz_sem.at[d - 1, 1], z_peer(d))
+    for d in range(1, blks):
+        go(txt.at[b], txt.at[b], tb_sem.at[d - 1], blk_peer(d))
+    for d in range(1, zs):
         go(w_hbm.at[mine], w_full.at[z, c, mine], wz_sem.at[d - 1], z_peer(d))
 
-    loads[0].wait()
+    loads[2].wait()
     for t in range(zs):
         turned = heads_ref[:, t * wide:(t + 1) * wide].T
         heads_t[0, t] = turned[:rows]
         heads_t[1, t] = turned[rows:]
     go(heads_t.at[1 - c], heads_peer, core_sem.at[1], partner)
 
-    loads[1].wait()
-    loads[2].wait()
-    image_units, image_scale = unit_rows(pic_ref[...])
-    text_units, text_scale = unit_rows(cap_ref[...])
-    img[c, z] = image_units.astype(bf16)
-    txt[b] = text_units.astype(bf16)
-    for d in range(1, zs):
-        go(img.at[c, z], img.at[c, z], iz_sem.at[d - 1, 0], z_peer(d))
-        go(img_ids.at[c, z], img_ids.at[c, z], iz_sem.at[d - 1, 1], z_peer(d))
-    for d in range(1, blks):
-        go(txt.at[b], txt.at[b], tb_sem.at[d - 1], blk_peer(d))
-    go(w_hbm, w_full.at[z, c], wc_sem.at[0], partner)
-
     loads[3].wait()
     arrived(adj_peer, core_sem.at[0])
     arrived(heads_peer, core_sem.at[1])
-    tile = cols // 3 if cols % 384 == 0 else cols
-    for k in range(zs):
-        t = z_of(k + 1)
-        for j in range(0, cols, tile):
-            part[k, :, j:j + tile] = (
-                jnp.dot(heads_t[c, t], adj_ref[:, j:j + tile], preferred_element_type=f32)
-                + jnp.dot(heads_peer[t], adj_peer[:, j:j + tile], preferred_element_type=f32)
-            ).astype(bf16)
-        f = 1 + k % 2
-        to = (flip[f], g)
-        go(part.at[k, rows_of(flip[3])], first_in.at[k, 1], first_sem.at[k, 1], to)
-        go(part.at[k, rows_of(flip[f])], first_in.at[k, 0], first_sem.at[k, 0], to)
+    half = cols // 2
+    for h in range(2):
+        for k in range(zs):
+            t = z_of(k + 1)
+            for j in range(0, half, 256):
+                at = h * half + j
+                part[h, k, :, j:j + 256] = (
+                    jnp.dot(heads_t[c, t], adj_ref[:, at:at + 256], preferred_element_type=f32)
+                    + jnp.dot(heads_peer[t], adj_peer[:, at:at + 256], preferred_element_type=f32)
+                ).astype(bf16)
+            f = 1 + (h + k) % 2
+            to = (flip[f], g)
+            go(part.at[h, k, rows_of(flip[3])], first_in.at[h, k, 1], first_sem.at[h, k, 1], to)
+            go(part.at[h, k, rows_of(flip[f])], first_in.at[h, k, 0], first_sem.at[h, k, 0], to)
+    go(w_hbm, w_full.at[z, c], wc_sem.at[0], partner)
 
     for d in range(1, zs):
         arrived(img.at[c, z_of(-d)], iz_sem.at[d - 1, 0])
         arrived(img_ids.at[c, z_of(-d)], iz_sem.at[d - 1, 1])
     go(img.at[c], img.at[c], core_sem.at[2], partner)
     go(img_ids.at[c], img_ids.at[c], core_sem.at[3], partner)
-
-    half = cols // 2
 
     def w_piece(e, i, h):
         return w_full.at[z_of(-e), c, rows_of(i), h * half:(h + 1) * half]
@@ -336,27 +335,42 @@
             adj_ref[...], both, (((1,), (1,)), ((), ())), preferred_element_type=f32
         ).astype(bf16)
 
-    def step_two(k):
-        s = 2 - k % 2
-        arrived(first_in.at[k, 1], first_sem.at[k, 1])
-        second[k] = (
-            part[k, rows_of(flip[s])].astype(f32) + first_in[k, 1].astype(f32)
+    def step_two(h, k):
+        s = 2 - (h + k) % 2
+        arrived(first_in.at[h, k, 1], first_sem.at[h, k, 1])
+        second[h, k] = (
+            part[h, k, rows_of(flip[s])].astype(f32) + first_in[h, k, 1].astype(f32)
         ).astype(bf16)
-        go(second.at[k], second_in.at[k], second_sem.at[k], (flip[s], g))
-
-    def step_three(k):
-        arrived(first_in.at[k, 0], first_sem.at[k, 0])
-        arrived(second_in.at[k], second_sem.at[k])
+        go(second.at[h, k], second_in.at[h, k], second_sem.at[h, k], (flip[s], g))
+
+    def step_three(h, k):
+        arrived(first_in.at[h, k, 0], first_sem.at[h, k, 0])
+        arrived(second_in.at[h, k], second_sem.at[h, k])
         total = (
-            part[k, mine].astype(f32) + first_in[k, 0].astype(f32) + second_in[k].astype(f32)
+            part[h, k, mine].astype(f32)
+            + first_in[h, k, 0].astype(f32)
+            + second_in[h, k].astype(f32)
         )
         if k < zs - 1:
-            zsum[k] = total.astype(bf16)
-            go(zsum.at[k], zsum_in.at[k], zsum_sem.at[k], z_peer(k + 1))
+            zsum[h, k] = total.astype(bf16)
+            go(zsum.at[h, k], zsum_in.at[h, k], zsum_sem.at[h, k], z_peer(k + 1))
         return total
 
-    loads[4].wait()
-    own_attn(0)
+    def finish(h, total):
+        for k in range(zs - 1):
+            arrived(zsum_in.at[h, k], zsum_sem.at[h, k])
+            total += zsum_in[h, k].astype(f32)
+        done[h, 0] = (total * scale).astype(bf16)
+        for d in range(1, blks):
+            go(done.at[h, 0], done.at[h, d], done_sem.at[h, d - 1], blk_peer(d))
+
+    w_first(1)
+    for k in range(zs):
+        step_two(0, k)
+    for e in range(2, zs):
+        w_first(e)
+    for k in range(zs):
+        step_two(1, k)
 
     for d in range(1, blks):
         arrived(txt.at[lax.rem(b + blks - d, blks)], tb_sem.at[d - 1])
@@ -386,32 +400,27 @@
         to = blk_peer(d)
         go(txt_part.at[to[0]], txt_in.at[d - 1], tr_sem.at[d - 1], to)
 
-    w_first(1)
-    step_two(0)
-    step_two(1)
-    for e in range(2, zs):
-        w_first(e)
-        step_two(e)
+    for k in range(zs):
+        total_a = step_three(0, k)
+        if k == 1:
+            w_second(1)
     arrived(img_core_in, core_sem.at[4])
     img_z[...] = img_part[c] + img_core_in[...]
     for d in range(1, zs):
         go(img_z.at[z_of(d)], img_z_in.at[d - 1], ir_sem.at[d - 1], z_peer(d))
     for k in range(zs):
-        total = step_three(k)
-        if 1 <= k:
+        total_b = step_three(1, k)
+        if 1 < k:
             w_second(k)
-
-    for k in range(zs - 1):
-        arrived(zsum_in.at[k], zsum_sem.at[k])
-        total += zsum_in[k].astype(f32)
-    done[0] = (total * scale).astype(bf16)
-    for d in range(1, blks):
-        go(done.at[0], done.at[d], done_sem.at[d - 1], blk_peer(d))
-
-    for e in range(1, zs):
+    loads[4].wait()
+    own_attn(0)
+
+    finish(0, total_a)
+    w_core(1)
+    finish(1, total_b)
+    for e in range(2, zs):
         w_core(e)
-        if e > 1:
-            own_attn(e - 1)
+        own_attn(e - 1)
 
     image_grad = img_z[z]
     for d in range(1, zs):
@@ -425,13 +434,23 @@
     cap_out[...] = back_through_norm(text_units, text_scale, text_grad)
 
     own_attn(zs - 1)
-    wgrad_out[mine] = done[0].astype(f32)
-    for d in range(1, blks):
-        arrived(done.at[d], done_sem.at[d - 1])
-        wgrad_out[rows_of(lax.rem(b + blks - d, blks))] = done[d].astype(f32)
+    for h in range(2):
+        span = slice(h * half, (h + 1) * half)
+        wgrad_out[mine, span] = done[h, 0].astype(f32)
+        for d in range(1, blks):
+            arrived(done.at[h, d], done_sem.at[h, d - 1])
+            wgrad_out[rows_of(lax.rem(b + blks - d, blks)), span] = done[h, d].astype(f32)
 
     for copy in sent:
         copy.wait_send()
+
+
+def store_kernel(*refs):
+    copies = [pltpu.make_async_copy(refs[i], refs[4 + i], refs[8].at[i]) for i in range(4)]
+    for copy in copies:
+        copy.start()
+    for copy in copies:
+        copy.wait()
 
 
 def fused_device(blks, grps, pic, cap, ids, sharp, bias, heads, adj, w):
@@ -440,12 +459,13 @@
     tokens, cols = adj.shape
     rows = w.shape[0]
     chunk = rows // blks
+    half = cols // 2
     scale = 1.0 / math.sqrt(tokens * blks * grps)
     vmem = pl.BlockSpec(memory_space=pltpu.VMEM)
     smem = pl.BlockSpec(memory_space=pltpu.SMEM)
-    hbm = pl.BlockSpec(memory_space=pl.ANY)
+    hbm = pl.BlockSpec(memory_space=pltpu.HBM)
     dma = pltpu.SemaphoreType.DMA
-    return pl.pallas_call(
+    grads = pl.pallas_call(
         functools.partial(fused_kernel, blks, zs, scale),
         out_shape=(
             jax.ShapeDtypeStruct(pic.shape, f32),
@@ -464,13 +484,13 @@
             pltpu.VMEM((zs, rows, tokens), bf16),
             pltpu.VMEM((tokens, cols), bf16),
             pltpu.VMEM((zs, 2, rows, cols), bf16),
-            pltpu.VMEM((zs, rows, cols), bf16),
-            pltpu.VMEM((zs, 2, chunk, cols), bf16),
-            pltpu.VMEM((zs, chunk, cols), bf16),
-            pltpu.VMEM((zs, chunk, cols), bf16),
-            pltpu.VMEM((zs - 1, chunk, cols), bf16),
-            pltpu.VMEM((zs - 1, chunk, cols), bf16),
-            pltpu.VMEM((blks, chunk, cols), bf16),
+            pltpu.VMEM((2, zs, rows, half), bf16),
+            pltpu.VMEM((2, zs, 2, chunk, half), bf16),
+            pltpu.VMEM((2, zs, chunk, half), bf16),
+            pltpu.VMEM((2, zs, chunk, half), bf16),
+            pltpu.VMEM((2, zs - 1, chunk, half), bf16),
+            pltpu.VMEM((2, zs - 1, chunk, half), bf16),
+            pltpu.VMEM((2, blks, chunk, half), bf16),
             pltpu.VMEM((2, zs, own, width), bf16),
             pltpu.VMEM((2, zs, own, 128), jnp.int32),
             pltpu.VMEM((blks, own, width), bf16),
@@ -486,22 +506,30 @@
             dma((zs - 1, 2, 2)),
             dma((zs - 1, 2, 2, 2)),
             dma((zs, 2)),
-            dma((zs, 2, 2)),
-            dma((zs, 2)),
-            dma((zs - 1, 2)),
-            dma((blks - 1, 2)),
+            dma((2, zs, 2, 2)),
+            dma((2, zs, 2)),
+            dma((2, zs - 1, 2)),
+            dma((2, blks - 1, 2)),
             dma((zs - 1, 2, 2)),
             dma((blks - 1, 2)),
             dma((zs - 1, 2)),
             dma((blks - 1, 2)),
         ],
         compiler_params=pltpu.CompilerParams(
-            collective_id=0, has_side_effects=True, vmem_limit_bytes=56 * 1024 * 1024
+            collective_id=0, has_side_effects=True, vmem_limit_bytes=50 * 1024 * 1024
         ),
         cost_estimate=pl.CostEstimate(
             flops=4 * tokens * cols * cols, bytes_accessed=8 * tokens * cols, transcendentals=0
         ),
     )(sharp, bias, ids, pic, cap, heads, adj, w)
+    anywhere = pl.BlockSpec(memory_space=pl.ANY)
+    return pl.pallas_call(
+        store_kernel,
+        out_shape=tuple(jax.ShapeDtypeStruct(x.shape, x.dtype) for x in grads),
+        in_specs=[anywhere] * 4,
+        out_specs=(anywhere,) * 4,
+        scratch_shapes=[dma((4,))],
+    )(*grads)
 
 
 def per_device(pic, cap, ids, sharp, bias, heads, adj, w):
@@ -518,7 +546,7 @@
         and heads.shape[1] == rows * grps
         and cols == heads.shape[1]
         and own % 16 == 0
-        and cols % 256 == 0
+        and cols % 512 == 0
     )
     if not fits:
         return plain_device(pic, cap, ids, sharp, bias, heads, adj, w)

time: 69 us -> 143 us (2.07)
  Pallas kernels: 60.3 us -> 134 us
    pallas_call x0 -> x1, Pallas kernels: none -> 77.1 us  [fused_device(): pl.pallas_call(store_kernel, out_shape=tuple((jax.ShapeDtypeStruct(x.shap...]
    pallas_call x1, Pallas kernels: 60.3 us -> 56.6 us  [fused_device(): pl.pallas_call(functools.partial(fused_kernel, blks, zs, scale), out_shap...]
    unnamed x6 -> x16, local copies, waits for them, and re-layouts: 6.51 us -> 6.8 us
where the time goes in v2:
time: 143 us; the launch traced here: 142 us
  Pallas kernels  134 us (94%)
  local copies, waits for them, and re-layouts  6.8 us (5%)
  between operations  1.95 us (1%)
    pallas_call x1, Pallas kernels, fused_device(): pl.pallas_call(store_kernel, out_shape=tuple((jax.ShapeDtypeStruct(x.shap...  77.1 us
    pallas_call x1, Pallas kernels, fused_device(): pl.pallas_call(functools.partial(fused_kernel, blks, zs, scale), out_shap...  56.6 us
    unnamed x16, local copies, waits for them, and re-layouts  6.8 us

profile of v2, /device:TPU:0, one launch (start us, length us, event | category | flops | bytes accessed | tf_op | source)
XLA Modules:
  0.0 142.4 jit_solution(9380704025275050113)
XLA Ops:
  1.9 0.0 copy-start.4
  1.9 1.1 copy-done.4
  3.0 0.0 copy-start.5
  3.0 0.9 copy-done.5
  3.9 0.0 copy-start.6
  3.9 0.9 copy-done.6
  4.8 0.0 copy-start.7
  4.8 0.7 copy-done.7
  5.4 56.6 %shard_map.111 = (f32[16,1152]{1,0:T(8,128)S(1)}, f32[16,1152]{1,0:T(8,128)S(1)}, bf16[384,1536]{1,0:T(8,128)(2,1)S(1)}, f32[192,1536]{1,0:T(8,128)S(1)}) custom-call(f32[1]{0:T(128)S(6)} %copy.12.sharp_ref, f32[1]{0:T(128)S(6)} %copy.13.bias_ref, s32[16]{0:T(128)S(1)} %copy-done.7, f32[16,1152]{1,0:T(8,128)S(1)} %copy-done.5, f32[16,1152]{1,0:T(8,128)S(1)} %copy-done.6, ...), custom_call_target="tpu_custom_call" | custom-call | flops 3623878656 | bytes 4718592 | tf_op jit(solution)/shard_map/pallas_call | solution.py:468
  62.0 0.0 copy-start
  62.0 1.0 copy-done
  63.1 0.0 copy-start.1
  63.1 1.0 copy-done.1
  64.1 0.0 copy-start.2
  64.1 0.6 copy-done.2
  64.7 0.0 copy-start.3
  64.7 0.6 copy-done.3
  65.4 77.1 %shard_map.112 = (f32[16,1152]{1,0:T(8,128)}, f32[16,1152]{1,0:T(8,128)}, bf16[384,1536]{1,0:T(8,128)(2,1)}, f32[192,1536]{1,0:T(8,128)}) custom-call(f32[16,1152]{1,0:T(8,128)} %copy-done.2, f32[16,1152]{1,0:T(8,128)} %copy-done.3, bf16[384,1536]{1,0:T(8,128)(2,1)} %copy-done, f32[192,1536]{1,0:T(8,128)} %copy-done.1), custom_call_target="tpu_custom_call" | custom-call | tf_op jit(solution)/shard_map/pallas_call | solution.py:526
Async XLA Ops:
  1.9 1.1 copy-start.4
  3.0 0.9 copy-start.5
  3.9 0.9 copy-start.6
  4.8 0.7 copy-start.7
  62.0 1.0 copy-start
  63.1 1.0 copy-start.1
  64.1 0.6 copy-start.2
  64.7 0.6 copy-start.3

commit v3 on v2

--- a/solution.py
+++ b/solution.py
@@ -175,6 +175,7 @@
     txt_in,
     load_sem,
     core_sem,
+    turn_sem,
     wz_sem,
     w1_sem,
     w2_sem,
@@ -271,24 +272,25 @@
         go(w_hbm.at[mine], w_full.at[z, c, mine], wz_sem.at[d - 1], z_peer(d))
 
     loads[2].wait()
-    for t in range(zs):
-        turned = heads_ref[:, t * wide:(t + 1) * wide].T
-        heads_t[0, t] = turned[:rows]
-        heads_t[1, t] = turned[rows:]
-    go(heads_t.at[1 - c], heads_peer, core_sem.at[1], partner)
+    for k in range(zs):
+        t = z_of(k + 1)
+        turned = heads_ref[:, pl.ds(pl.multiple_of(t * wide, 128), wide)].T
+        heads_t[0, k] = turned[:rows]
+        heads_t[1, k] = turned[rows:]
+        go(heads_t.at[1 - c, k], heads_peer.at[k], turn_sem.at[k], partner)
 
     loads[3].wait()
     arrived(adj_peer, core_sem.at[0])
-    arrived(heads_peer, core_sem.at[1])
     half = cols // 2
     for h in range(2):
         for k in range(zs):
-            t = z_of(k + 1)
+            if h == 0:
+                arrived(heads_peer.at[k], turn_sem.at[k])
             for j in range(0, half, 256):
                 at = h * half + j
                 part[h, k, :, j:j + 256] = (
-                    jnp.dot(heads_t[c, t], adj_ref[:, at:at + 256], preferred_element_type=f32)
-                    + jnp.dot(heads_peer[t], adj_peer[:, at:at + 256], preferred_element_type=f32)
+                    jnp.dot(heads_t[c, k], adj_ref[:, at:at + 256], preferred_element_type=f32)
+                    + jnp.dot(heads_peer[k], adj_peer[:, at:at + 256], preferred_element_type=f32)
                 ).astype(bf16)
             f = 1 + (h + k) % 2
             to = (flip[f], g)
@@ -446,11 +448,8 @@
 
 
 def store_kernel(*refs):
-    copies = [pltpu.make_async_copy(refs[i], refs[4 + i], refs[8].at[i]) for i in range(4)]
-    for copy in copies:
-        copy.start()
-    for copy in copies:
-        copy.wait()
+    for i in range(4):
+        refs[4 + i][...] = refs[i][...]
 
 
 def fused_device(blks, grps, pic, cap, ids, sharp, bias, heads, adj, w):
@@ -502,6 +501,7 @@
             pltpu.VMEM((blks - 1, own, width), f32),
             dma((5,)),
             dma((5, 2)),
+            dma((zs, 2)),
             dma((zs - 1, 2)),
             dma((zs - 1, 2, 2)),
             dma((zs - 1, 2, 2, 2)),
@@ -522,13 +522,11 @@
             flops=4 * tokens * cols * cols, bytes_accessed=8 * tokens * cols, transcendentals=0
         ),
     )(sharp, bias, ids, pic, cap, heads, adj, w)
-    anywhere = pl.BlockSpec(memory_space=pl.ANY)
     return pl.pallas_call(
         store_kernel,
         out_shape=tuple(jax.ShapeDtypeStruct(x.shape, x.dtype) for x in grads),
-        in_specs=[anywhere] * 4,
-        out_specs=(anywhere,) * 4,
-        scratch_shapes=[dma((4,))],
+        in_specs=[vmem] * 4,
+        out_specs=(vmem,) * 4,
     )(*grads)
 
 

time: 143 us -> 68.5 us (0.48)
  Pallas kernels: 134 us -> 59.5 us
    pallas_call x1, Pallas kernels: 77.1 us -> 3.2 us  [fused_device(): pl.pallas_call(store_kernel, out_shape=tuple((jax.ShapeDtypeStruct(x.shap...]
where the time goes in v3:
time: 68.5 us; the launch traced here: 68.2 us
  Pallas kernels  59.5 us (87%)
  local copies, waits for them, and re-layouts  6.8 us (10%)
  between operations  1.95 us (3%)
    pallas_call x1, Pallas kernels, fused_device(): pl.pallas_call(functools.partial(fused_kernel, blks, zs, scale), out_shap...  56.3 us
    unnamed x16, local copies, waits for them, and re-layouts  6.8 us
    pallas_call x1, Pallas kernels, fused_device(): pl.pallas_call(store_kernel, out_shape=tuple((jax.ShapeDtypeStruct(x.shap...  3.2 us

profile of v3, /device:TPU:0, one launch (start us, length us, event | category | flops | bytes accessed | tf_op | source)
XLA Modules:
  0.0 68.2 jit_solution(11867616712536263433)
XLA Ops:
  1.9 0.0 copy-start.4
  1.9 1.1 %copy-done.4 = bf16[192,1536]{1,0:T(8,128)(2,1)S(1)} copy-done((bf16[192,1536]{1,0:T(8,128)(2,1)S(1)}, bf16[192,1536]{1,0:T(8,128)(2,1)}, u32[]{:S(2)}) %copy-start.4) | copy-done | bytes 589848
  3.0 0.0 copy-start.5
  3.0 0.9 %copy-done.5 = f32[16,1152]{1,0:T(8,128)S(1)} copy-done((f32[16,1152]{1,0:T(8,128)S(1)}, f32[16,1152]{1,0:T(8,128)}, u32[]{:S(2)}) %copy-start.5) | copy-done | bytes 73752
  3.9 0.0 copy-start.6
  3.9 0.9 %copy-done.6 = f32[16,1152]{1,0:T(8,128)S(1)} copy-done((f32[16,1152]{1,0:T(8,128)S(1)}, f32[16,1152]{1,0:T(8,128)}, u32[]{:S(2)}) %copy-start.6) | copy-done | bytes 73752
  4.8 0.0 copy-start.7
  4.8 0.7 copy-done.7
  5.4 56.3 %shard_map.111 = (f32[16,1152]{1,0:T(8,128)S(1)}, f32[16,1152]{1,0:T(8,128)S(1)}, bf16[384,1536]{1,0:T(8,128)(2,1)S(1)}, f32[192,1536]{1,0:T(8,128)S(1)}) custom-call(f32[1]{0:T(128)S(6)} %copy.12.sharp_ref, f32[1]{0:T(128)S(6)} %copy.13.bias_ref, s32[16]{0:T(128)S(1)} %copy-done.7, f32[16,1152]{1,0:T(8,128)S(1)} %copy-done.5, f32[16,1152]{1,0:T(8,128)S(1)} %copy-done.6, ...), custom_call_target="tpu_custom_call" | custom-call | flops 3623878656 | bytes 4718592 | tf_op jit(solution)/shard_map/pallas_call | solution.py:467
  61.7 0.0 copy-start
  61.7 1.0 %copy-done = bf16[384,1536]{1,0:T(8,128)(2,1)} copy-done((bf16[384,1536]{1,0:T(8,128)(2,1)}, bf16[384,1536]{1,0:T(8,128)(2,1)S(1)}, u32[]{:S(2)}) %copy-start) | copy-done | bytes 1179672
  62.7 0.0 copy-start.1
  62.7 1.0 %copy-done.1 = f32[192,1536]{1,0:T(8,128)} copy-done((f32[192,1536]{1,0:T(8,128)}, f32[192,1536]{1,0:T(8,128)S(1)}, u32[]{:S(2)}) %copy-start.1) | copy-done | bytes 1179672
  63.8 0.0 copy-start.2
  63.8 0.6 copy-done.2
  64.4 0.0 copy-start.3
  64.4 0.6 copy-done.3
  65.0 3.2 %shard_map.112 = (f32[16,1152]{1,0:T(8,128)}, f32[16,1152]{1,0:T(8,128)}, bf16[384,1536]{1,0:T(8,128)(2,1)}, f32[192,1536]{1,0:T(8,128)}) custom-call(f32[16,1152]{1,0:T(8,128)} %copy-done.2, f32[16,1152]{1,0:T(8,128)} %copy-done.3, bf16[384,1536]{1,0:T(8,128)(2,1)} %copy-done, f32[192,1536]{1,0:T(8,128)} %copy-done.1), custom_call_target="tpu_custom_call" | custom-call | tf_op jit(solution)/shard_map/pallas_call | solution.py:525
Async XLA Ops:
  1.9 1.1 %copy-start.4 = (bf16[192,1536]{1,0:T(8,128)(2,1)S(1)}, bf16[192,1536]{1,0:T(8,128)(2,1)}, u32[]{:S(2)}) copy-start(bf16[192,1536]{1,0:T(8,128)(2,1)} %w_hbm.1) | copy-start | bytes 1769476
  3.0 0.9 %copy-start.5 = (f32[16,1152]{1,0:T(8,128)S(1)}, f32[16,1152]{1,0:T(8,128)}, u32[]{:S(2)}) copy-start(f32[16,1152]{1,0:T(8,128)} %pic_hbm.1) | copy-start | bytes 221188
  3.9 0.9 %copy-start.6 = (f32[16,1152]{1,0:T(8,128)S(1)}, f32[16,1152]{1,0:T(8,128)}, u32[]{:S(2)}) copy-start(f32[16,1152]{1,0:T(8,128)} %cap_hbm.1) | copy-start | bytes 221188
  4.8 0.7 copy-start.7
  61.7 1.0 %copy-start = (bf16[384,1536]{1,0:T(8,128)(2,1)}, bf16[384,1536]{1,0:T(8,128)(2,1)S(1)}, u32[]{:S(2)}) copy-start(bf16[384,1536]{1,0:T(8,128)(2,1)S(1)} %get-tuple-element.10.refs_2_) | copy-start | bytes 3538948
  62.7 1.0 %copy-start.1 = (f32[192,1536]{1,0:T(8,128)}, f32[192,1536]{1,0:T(8,128)S(1)}, u32[]{:S(2)}) copy-start(f32[192,1536]{1,0:T(8,128)S(1)} %get-tuple-element.11.refs_3_) | copy-start | bytes 3538948
  63.8 0.6 copy-start.2
  64.4 0.6 copy-start.3

commit v4 on v3

--- a/solution.py
+++ b/solution.py
@@ -177,6 +177,7 @@
     core_sem,
     turn_sem,
     wz_sem,
+    ws_sem,
     w1_sem,
     w2_sem,
     wc_sem,
@@ -268,8 +269,17 @@
         go(img_ids.at[c, z], img_ids.at[c, z], iz_sem.at[d - 1, 1], z_peer(d))
     for d in range(1, blks):
         go(txt.at[b], txt.at[b], tb_sem.at[d - 1], blk_peer(d))
+    z_cols = 128 * (cols // 768)
+    z_cols += (cols - z_cols) % 256
+    span = (cols - z_cols) // 2
+    rest = pl.ds(z_cols, 2 * span)
+    straight = pl.ds(0, z_cols)
     for d in range(1, zs):
-        go(w_hbm.at[mine], w_full.at[z, c, mine], wz_sem.at[d - 1], z_peer(d))
+        go(w_hbm.at[mine, rest], w_full.at[z, c, mine, rest], wz_sem.at[d - 1], z_peer(d))
+    for d in range(1, zs):
+        go(
+            w_hbm.at[:, straight], w_full.at[z, c, :, straight], ws_sem.at[d - 1], z_peer(d)
+        )
 
     loads[2].wait()
     for k in range(zs):
@@ -305,10 +315,10 @@
     go(img_ids.at[c], img_ids.at[c], core_sem.at[3], partner)
 
     def w_piece(e, i, h):
-        return w_full.at[z_of(-e), c, rows_of(i), h * half:(h + 1) * half]
+        return w_full.at[z_of(-e), c, rows_of(i), pl.ds(z_cols + h * span, span)]
 
     def w_first(e):
-        arrived(w_full.at[z_of(-e), c, mine], wz_sem.at[e - 1])
+        arrived(w_full.at[z_of(-e), c, mine, rest], wz_sem.at[e - 1])
         for h in range(2):
             piece = w_piece(e, b, h)
             go(piece, piece, w1_sem.at[e - 1, h], (flip[1 + h], g))
@@ -323,6 +333,7 @@
             go(piece, piece, w2_sem.at[e - 1, h, 1], to)
 
     def w_core(e):
+        arrived(w_full.at[z_of(-e), c, :, straight], ws_sem.at[e - 1])
         for h in range(2):
             arrived(w_piece(e, flip[3], h), w2_sem.at[e - 1, h, 0])
             arrived(w_piece(e, flip[2 - h], h), w2_sem.at[e - 1, h, 1])
@@ -437,19 +448,27 @@
 
     own_attn(zs - 1)
     for h in range(2):
-        span = slice(h * half, (h + 1) * half)
-        wgrad_out[mine, span] = done[h, 0].astype(f32)
+        side = slice(h * half, (h + 1) * half)
+        wgrad_out[mine, side] = done[h, 0].astype(f32)
         for d in range(1, blks):
             arrived(done.at[h, d], done_sem.at[h, d - 1])
-            wgrad_out[rows_of(lax.rem(b + blks - d, blks)), span] = done[h, d].astype(f32)
+            wgrad_out[rows_of(lax.rem(b + blks - d, blks)), side] = done[h, d].astype(f32)
 
     for copy in sent:
         copy.wait_send()
 
 
 def store_kernel(*refs):
-    for i in range(4):
-        refs[4 + i][...] = refs[i][...]
+    ins, outs, held, sems = refs[:4], refs[4:8], refs[8:12], refs[12]
+    loads = [pltpu.make_async_copy(ins[i], held[i], sems.at[0, i]) for i in range(4)]
+    stores = [pltpu.make_async_copy(held[i], outs[i], sems.at[1, i]) for i in range(4)]
+    for load in loads:
+        load.start()
+    for load, store in zip(loads, stores):
+        load.wait()
+        store.start()
+    for store in stores:
+        store.wait()
 
 
 def fused_device(blks, grps, pic, cap, ids, sharp, bias, heads, adj, w):
@@ -503,6 +522,7 @@
             dma((5, 2)),
             dma((zs, 2)),
             dma((zs - 1, 2)),
+            dma((zs - 1, 2)),
             dma((zs - 1, 2, 2)),
             dma((zs - 1, 2, 2, 2)),
             dma((zs, 2)),
@@ -516,7 +536,7 @@
             dma((blks - 1, 2)),
         ],
         compiler_params=pltpu.CompilerParams(
-            collective_id=0, has_side_effects=True, vmem_limit_bytes=50 * 1024 * 1024
+            collective_id=0, has_side_effects=True, vmem_limit_bytes=56 * 1024 * 1024
         ),
         cost_estimate=pl.CostEstimate(
             flops=4 * tokens * cols * cols, bytes_accessed=8 * tokens * cols, transcendentals=0
@@ -525,8 +545,10 @@
     return pl.pallas_call(
         store_kernel,
         out_shape=tuple(jax.ShapeDtypeStruct(x.shape, x.dtype) for x in grads),
-        in_specs=[vmem] * 4,
-        out_specs=(vmem,) * 4,
+        in_specs=[hbm] * 4,
+        out_specs=(hbm,) * 4,
+        scratch_shapes=[pltpu.VMEM(x.shape, x.dtype) for x in grads] + [dma((2, 4))],
+        compiler_params=pltpu.CompilerParams(vmem_limit_bytes=56 * 1024 * 1024),
     )(*grads)
 
 

time: 68.5 us -> 60.9 us (0.89)
  local copies, waits for them, and re-layouts: 6.8 us -> 0 us
  Pallas kernels: 59.5 us -> 58.8 us
    unnamed x16 -> x0, local copies, waits for them, and re-layouts: 6.8 us -> none
where the time goes in v4:
time: 60.9 us; the launch traced here: 60.7 us
  Pallas kernels  58.8 us (97%)
  between operations  1.93 us (3%)
    pallas_call x1, Pallas kernels, fused_device(): pl.pallas_call(functools.partial(fused_kernel, blks, zs, scale), out_shap...  55.9 us
    pallas_call x1, Pallas kernels, fused_device(): pl.pallas_call(store_kernel, out_shape=tuple((jax.ShapeDtypeStruct(x.shap...  2.83 us

profile of v4, /device:TPU:0, one launch (start us, length us, event | category | flops | bytes accessed | tf_op | source)
XLA Modules:
  0.0 60.7 jit_solution(15610433390693985777)
XLA Ops:
  1.9 55.9 %shard_map.111 = (f32[16,1152]{1,0:T(8,128)}, f32[16,1152]{1,0:T(8,128)}, bf16[384,1536]{1,0:T(8,128)(2,1)}, f32[192,1536]{1,0:T(8,128)}) custom-call(f32[1]{0:T(128)S(6)} %copy.12.sharp_ref, f32[1]{0:T(128)S(6)} %copy.13.bias_ref, s32[16]{0:T(128)} %ids_ref.1, f32[16,1152]{1,0:T(8,128)} %pic_hbm.1, f32[16,1152]{1,0:T(8,128)} %cap_hbm.1, ...), custom_call_target="tpu_custom_call" | custom-call | flops 3623878656 | bytes 4718592 | tf_op jit(solution)/shard_map/pallas_call | solution.py:486
  57.9 2.8 %shard_map.112 = (f32[16,1152]{1,0:T(8,128)}, f32[16,1152]{1,0:T(8,128)}, bf16[384,1536]{1,0:T(8,128)(2,1)}, f32[192,1536]{1,0:T(8,128)}) custom-call(f32[16,1152]{1,0:T(8,128)} %get-tuple-element.8.refs_0_, f32[16,1152]{1,0:T(8,128)} %get-tuple-element.9.refs_1_, bf16[384,1536]{1,0:T(8,128)(2,1)} %get-tuple-element.10.refs_2_, ...), custom_call_target="tpu_custom_call" | custom-call | tf_op jit(solution)/shard_map/pallas_call | solution.py:545

commit v5 on v4

--- a/solution.py
+++ b/solution.py
@@ -147,6 +147,8 @@
     w_hbm,
     pic_out,
     cap_out,
+    attn_hbm,
+    wgrad_hbm,
     attn_out,
     wgrad_out,
     pic_ref,
@@ -189,6 +191,8 @@
     tb_sem,
     ir_sem,
     tr_sem,
+    attn_sem,
+    wgrad_sem,
 ):
     b = lax.axis_index("blk")
     g = lax.axis_index("grp")
@@ -314,6 +318,13 @@
     go(img.at[c], img.at[c], core_sem.at[2], partner)
     go(img_ids.at[c], img_ids.at[c], core_sem.at[3], partner)
 
+    kept = []
+
+    def keep(src, dst, sem):
+        copy = pltpu.make_async_copy(src, dst, sem)
+        copy.start()
+        kept.append(copy)
+
     def w_piece(e, i, h):
         return w_full.at[z_of(-e), c, rows_of(i), pl.ds(z_cols + h * span, span)]
 
@@ -344,9 +355,11 @@
         zf = z_of(-e)
         arrived(w_full.at[zf, 1 - c], wc_sem.at[e])
         both = w_full[zf].reshape(wide, cols)
-        attn_out[:, pl.ds(pl.multiple_of(zf * wide, 128), wide)] = lax.dot_general(
+        block = pl.ds(pl.multiple_of(zf * wide, 128), wide)
+        attn_out[:, block] = lax.dot_general(
             adj_ref[...], both, (((1,), (1,)), ((), ())), preferred_element_type=f32
         ).astype(bf16)
+        keep(attn_out.at[:, block], attn_hbm.at[:, block], attn_sem.at[e])
 
     def step_two(h, k):
         s = 2 - (h + k) % 2
@@ -449,19 +462,30 @@
     own_attn(zs - 1)
     for h in range(2):
         side = slice(h * half, (h + 1) * half)
-        wgrad_out[mine, side] = done[h, 0].astype(f32)
-        for d in range(1, blks):
-            arrived(done.at[h, d], done_sem.at[h, d - 1])
-            wgrad_out[rows_of(lax.rem(b + blks - d, blks)), side] = done[h, d].astype(f32)
+        for d in range(blks):
+            if d > 0:
+                arrived(done.at[h, d], done_sem.at[h, d - 1])
+            there = rows_of(lax.rem(b + blks - d, blks))
+            wgrad_out[there, side] = done[h, d].astype(f32)
+            keep(wgrad_out.at[there, side], wgrad_hbm.at[there, side], wgrad_sem.at[h, d])
 
     for copy in sent:
         copy.wait_send()
+    for copy in kept:
+        copy.wait()
 
 
 def store_kernel(*refs):
     ins, outs, held, sems = refs[:4], refs[4:8], refs[8:12], refs[12]
-    loads = [pltpu.make_async_copy(ins[i], held[i], sems.at[0, i]) for i in range(4)]
-    stores = [pltpu.make_async_copy(held[i], outs[i], sems.at[1, i]) for i in range(4)]
+    pieces = []
+    for i in (2, 3, 0, 1):
+        size = ins[i].shape[0]
+        step = size // 4 if size % 64 == 0 else size
+        pieces += [(i, pl.ds(at, step)) for at in range(0, size, step)]
+    loads, stores = [], []
+    for n, (i, at) in enumerate(pieces):
+        loads.append(pltpu.make_async_copy(ins[i].at[at], held[i].at[at], sems.at[0, n]))
+        stores.append(pltpu.make_async_copy(held[i].at[at], outs[i].at[at], sems.at[1, n]))
     for load in loads:
         load.start()
     for load, store in zip(loads, stores):
@@ -492,8 +516,10 @@
             jax.ShapeDtypeStruct(w.shape, f32),
         ),
         in_specs=[smem] * 3 + [hbm] * 5,
-        out_specs=(vmem,) * 4,
+        out_specs=(vmem, vmem, hbm, hbm),
         scratch_shapes=[
+            pltpu.VMEM(heads.shape, bf16),
+            pltpu.VMEM(w.shape, f32),
             pltpu.VMEM(pic.shape, f32),
             pltpu.VMEM(cap.shape, f32),
             pltpu.VMEM((tokens, cols), bf16),
@@ -534,6 +560,8 @@
             dma((blks - 1, 2)),
             dma((zs - 1, 2)),
             dma((blks - 1, 2)),
+            dma((zs,)),
+            dma((2, blks)),
         ],
         compiler_params=pltpu.CompilerParams(
             collective_id=0, has_side_effects=True, vmem_limit_bytes=56 * 1024 * 1024
@@ -547,7 +575,7 @@
         out_shape=tuple(jax.ShapeDtypeStruct(x.shape, x.dtype) for x in grads),
         in_specs=[hbm] * 4,
         out_specs=(hbm,) * 4,
-        scratch_shapes=[pltpu.VMEM(x.shape, x.dtype) for x in grads] + [dma((2, 4))],
+        scratch_shapes=[pltpu.VMEM(x.shape, x.dtype) for x in grads] + [dma((2, 16))],
         compiler_params=pltpu.CompilerParams(vmem_limit_bytes=56 * 1024 * 1024),
     )(*grads)
 

time: 60.9 us -> 60.7 us (level)
  no operation moved by 1% of the time
where the time goes in v5:
time: 60.7 us; the launch traced here: 60.5 us
  Pallas kernels  58.5 us (96%)
  between operations  1.93 us (3%)
    pallas_call x1, Pallas kernels, fused_device(): pl.pallas_call(functools.partial(fused_kernel, blks, zs, scale), out_shap...  55.9 us
    pallas_call x1, Pallas kernels, fused_device(): pl.pallas_call(store_kernel, out_shape=tuple((jax.ShapeDtypeStruct(x.shap...  2.68 us

profile of v5, /device:TPU:0, one launch (start us, length us, event | category | flops | bytes accessed | tf_op | source)
XLA Modules:
  0.0 60.5 jit_solution(15913369172147878591)
XLA Ops:
  1.9 55.9 %shard_map.111 = (f32[16,1152]{1,0:T(8,128)}, f32[16,1152]{1,0:T(8,128)}, bf16[384,1536]{1,0:T(8,128)(2,1)}, f32[192,1536]{1,0:T(8,128)}) custom-call(f32[1]{0:T(128)S(6)} %copy.12.sharp_ref, f32[1]{0:T(128)S(6)} %copy.13.bias_ref, s32[16]{0:T(128)} %ids_ref.1, f32[16,1152]{1,0:T(8,128)} %pic_hbm.1, f32[16,1152]{1,0:T(8,128)} %cap_hbm.1, ...), custom_call_target="tpu_custom_call" | custom-call | flops 3623878656 | bytes 4718592 | tf_op jit(solution)/shard_map/pallas_call | solution.py:510
  57.8 2.7 %shard_map.112 = (f32[16,1152]{1,0:T(8,128)}, f32[16,1152]{1,0:T(8,128)}, bf16[384,1536]{1,0:T(8,128)(2,1)}, f32[192,1536]{1,0:T(8,128)}) custom-call(f32[16,1152]{1,0:T(8,128)} %get-tuple-element.8.refs_0_, f32[16,1152]{1,0:T(8,128)} %get-tuple-element.9.refs_1_, bf16[384,1536]{1,0:T(8,128)(2,1)} %get-tuple-element.10.refs_2_, ...), custom_call_target="tpu_custom_call" | custom-call | tf_op jit(solution)/shard_map/pallas_call | solution.py:573
